TPU v7x, 32 devices: a whole 2x2x4 slice. The times are simulated.
32 devices in a mesh: batch: 16 (over z, y, x), tensor: 2 (over core).
Axes of the slice: x: 2, y: 2, z: 4, core: 2. Of those that a mesh axis runs over, the one named last changes fastest.
Arguments:
- tokens: bfloat16 [32768, 768], P('batch'), may hold values from -6 to 6
- lengths: int32 [64], P('batch'), may hold values from 64 to 512, as said below
- q_weight: float32 [768, 768], P('batch', 'tensor'), may hold values from -0.21875 to 0.21875
- k_weight: float32 [768, 768], P('batch', 'tensor'), may hold values from -0.21875 to 0.21875
- v_weight: float32 [768, 768], P('batch', 'tensor'), may hold values from -0.21875 to 0.21875
- output_weight: float32 [768, 768], P('tensor', 'batch'), may hold values from -0.875 to 0.875
- up_weight: float32 [768, 3072], P('batch', 'tensor'), may hold values from -0.21875 to 0.21875
- down_projection_weight: float32 [3072, 768], P('tensor', 'batch'), may hold values from -0.109375 to 0.109375
- q_bias: float32 [768], P('tensor'), may hold values from -3 to 3
- v_bias: float32 [768], P('tensor'), may hold values from -3 to 3
- o_bias: float32 [768], replicated, may hold values from -3 to 3
- up_bias: float32 [3072], P('tensor'), may hold values from -3 to 3
- down_bias: float32 [768], replicated, may hold values from -3 to 3
- gain_first: float32 [768], replicated, may hold values from 0.1 to 1.9
- shift_first: float32 [768], replicated, may hold values from -3 to 3
- gain_second: float32 [768], replicated, may hold values from 0.1 to 1.9
- shift_second: float32 [768], replicated, may hold values from -3 to 3
- out_grad: bfloat16 [32768, 768], P('batch'), may hold values from -6 to 6
Outputs:
- layer_out: bfloat16 [32768, 768], P('batch')
- tokens_grad: bfloat16 [32768, 768], P('batch')
- q_weight_grad: float32 [768, 768], P('batch', 'tensor')
- k_weight_grad: float32 [768, 768], P('batch', 'tensor')
- v_weight_grad: float32 [768, 768], P('batch', 'tensor')
- o_weight_grad: float32 [768, 768], P('tensor', 'batch')
- up_weight_grad: float32 [768, 3072], P('batch', 'tensor')
- down_weight_grad: float32 [3072, 768], P('tensor', 'batch')
- q_bias_grad: float32 [768], P('tensor')
- v_bias_grad: float32 [768], P('tensor')
- o_bias_grad: float32 [768], replicated
- up_bias_grad: float32 [3072], P('tensor')
- down_bias_grad: float32 [768], replicated
- gain_first_grad: float32 [768], replicated
- shift_first_grad: float32 [768], replicated
- gain_second_grad: float32 [768], replicated
- shift_second_grad: float32 [768], replicated
Inputs may be any that keep to these rules, and one draw needn't show every extreme that they name: lengths[s] is the number of real tokens of sequence s, which stand first; some sequence has exactly 512.
All inputs are finite; a program needn't handle non-finite values.
Results may differ from a plain program's by a relative error of at most 0.019.
Values may be sent and summed in bfloat16 or wider, within the bound.
No kernel may reach another device: no remote copies, remote signals or barrier semaphores. Data moves between devices by JAX's collectives and lax.ppermute only.
A program may use at most 128 MiB of HBM per device.

v0:
```python
import math

import jax
import jax.numpy as jnp
from jax import lax
from jax.sharding import PartitionSpec as P

HEAD_DIM = 64


EPSILON = 1e-12
NEGATIVE = -1000000000.0
HALF = jnp.bfloat16
SINGLE = jnp.float32


def matmul(left, right):
    return jnp.dot(left, right, preferred_element_type=SINGLE)


def inner_rows(left, right):
    return lax.dot_general(left, right, (((0,), (0,)), ((), ())), preferred_element_type=SINGLE)


def outer_cols(left, right):
    return lax.dot_general(left, right, (((1,), (1,)), ((), ())), preferred_element_type=SINGLE)


def layer_norm(values, gain, shift):
    center = values - jnp.mean(values, -1, keepdims=True)
    inverse = lax.rsqrt(jnp.mean(center * center, -1, keepdims=True) + EPSILON)
    normal = center * inverse
    return (normal * gain + shift, normal, inverse)


def norm_back(grad, normal, inverse, gain):
    scaled = grad * gain
    inner = (
        scaled
        - jnp.mean(scaled, -1, keepdims=True)
        - normal * jnp.mean(scaled * normal, -1, keepdims=True)
    )
    return (inner * inverse, jnp.sum(grad * normal, 0), jnp.sum(grad, 0))


def gelu_parts(upper):
    cdf = 0.5 * (1.0 + lax.erf(upper * (1.0 / math.sqrt(2.0))))
    density = jnp.exp(-0.5 * upper * upper) * (1.0 / math.sqrt(2.0 * math.pi))
    return (upper * cdf, cdf + upper * density)


def to_heads(flat, seq_count):
    rows, width = flat.shape
    return flat.reshape(seq_count, rows // seq_count, width // HEAD_DIM, HEAD_DIM).transpose(
        0, 2, 1, 3
    )


def from_heads(stacked):
    seq_count, heads_here, span, size = stacked.shape
    return stacked.transpose(0, 2, 1, 3).reshape(seq_count * span, heads_here * size)


def scores_of(query_seq, key_seq, mask):
    scores = jnp.einsum(
        "hqd,hkd->hqk", query_seq, key_seq, preferred_element_type=SINGLE
    ) * HEAD_DIM ** (-0.5)
    return jnp.where(mask[None, None, :], scores, NEGATIVE)


def attend_core(item):
    query_seq, key_seq, value_seq, mask = item
    scores = scores_of(query_seq, key_seq, mask)
    top = jnp.max(scores, -1, keepdims=True)
    expo = jnp.exp(scores - top)
    total = jnp.sum(expo, -1, keepdims=True)
    probs = expo / total
    mixed = jnp.einsum("hqk,hkd->hqd", probs.astype(HALF), value_seq, preferred_element_type=SINGLE)
    return (mixed, top + jnp.log(total), probs)


def attend_lse(item):
    mixed, log_total, probs = attend_core(item)
    return (mixed, log_total)


def attend_grads(probs, query_seq, key_seq, value_seq, out_grad):
    scale = HEAD_DIM ** (-0.5)
    value_grad = jnp.einsum(
        "hqk,hqd->hkd", probs.astype(HALF), out_grad, preferred_element_type=SINGLE
    )
    prob_grad = jnp.einsum("hqd,hkd->hqk", out_grad, value_seq, preferred_element_type=SINGLE)
    delta = jnp.sum(probs * prob_grad, -1, keepdims=True)
    score_grad = (probs * (prob_grad - delta)).astype(HALF)
    query_grad = (
        jnp.einsum("hqk,hkd->hqd", score_grad, key_seq, preferred_element_type=SINGLE) * scale
    )
    key_grad = (
        jnp.einsum("hqk,hqd->hkd", score_grad, query_seq, preferred_element_type=SINGLE) * scale
    )
    return (query_grad.astype(HALF), key_grad.astype(HALF), value_grad.astype(HALF))


def back_recompute(item):
    query_seq, key_seq, value_seq, mask, log_total, out_grad = item
    probs = jnp.exp(scores_of(query_seq, key_seq, mask) - log_total)
    return attend_grads(probs, query_seq, key_seq, value_seq, out_grad)


def per_device(
    tokens,
    lengths,
    q_weight,
    k_weight,
    v_weight,
    output_weight,
    up_weight,
    down_projection_weight,
    q_bias,
    v_bias,
    o_bias,
    up_bias,
    down_bias,
    gain_first,
    shift_first,
    gain_second,
    shift_second,
    out_grad,
):
    q_proj, k_proj, v_proj, o_proj, up_proj, down_proj = (
        lax.all_gather(q_weight.astype(HALF), "batch", axis=0, tiled=True),
        lax.all_gather(k_weight.astype(HALF), "batch", axis=0, tiled=True),
        lax.all_gather(v_weight.astype(HALF), "batch", axis=0, tiled=True),
        lax.all_gather(output_weight.astype(HALF), "batch", axis=1, tiled=True),
        lax.all_gather(up_weight.astype(HALF), "batch", axis=0, tiled=True),
        lax.all_gather(down_projection_weight.astype(HALF), "batch", axis=1, tiled=True),
    )
    seq_count = lengths.shape[0]
    rows = tokens.shape[0]
    span = rows // seq_count
    valid = jnp.arange(span, dtype=jnp.int32)[None, :] < lengths[:, None]
    inputs = tokens.astype(SINGLE)
    query = (matmul(tokens, q_proj) + q_bias).astype(HALF)
    keys = matmul(tokens, k_proj).astype(HALF)
    values = (matmul(tokens, v_proj) + v_bias).astype(HALF)
    query_heads = to_heads(query, seq_count)
    key_heads = to_heads(keys, seq_count)
    value_heads = to_heads(values, seq_count)
    mixed_heads, log_total = lax.map(attend_lse, (query_heads, key_heads, value_heads, valid))
    mixed = from_heads(mixed_heads).astype(HALF)
    attention_block = lax.psum(matmul(mixed, o_proj).astype(jnp.bfloat16), "tensor").astype(
        jnp.float32
    )
    normed_first, normal_first, inverse_first = layer_norm(
        inputs + attention_block + o_bias, gain_first, shift_first
    )
    normed_half = normed_first.astype(HALF)
    upper = matmul(normed_half, up_proj) + up_bias
    active_rows, slope = gelu_parts(upper)
    active_half = active_rows.astype(HALF)
    residual_branch = lax.psum(
        matmul(active_half, down_proj).astype(jnp.bfloat16), "tensor"
    ).astype(jnp.float32)
    output, normal_second, inverse_second = layer_norm(
        normed_first + residual_branch + down_bias, gain_second, shift_second
    )
    grad_second, gain_second_grad, shift_second_grad = norm_back(
        out_grad.astype(SINGLE), normal_second, inverse_second, gain_second
    )
    down_bias_grad = jnp.sum(grad_second, 0)
    grad_second_half = grad_second.astype(HALF)
    down_grad = inner_rows(active_half, grad_second_half)
    upper_grad = (outer_cols(grad_second_half, down_proj) * slope).astype(HALF)
    up_bias_grad = jnp.sum(upper_grad.astype(SINGLE), 0)
    up_grad = inner_rows(normed_half, upper_grad)
    normed_grad = grad_second + lax.psum(
        outer_cols(upper_grad, up_proj).astype(jnp.bfloat16), "tensor"
    ).astype(jnp.float32)
    grad_first, gain_first_grad, shift_first_grad = norm_back(
        normed_grad, normal_first, inverse_first, gain_first
    )
    o_bias_grad = jnp.sum(grad_first, 0)
    grad_first_half = grad_first.astype(HALF)
    o_grad = inner_rows(mixed, grad_first_half)
    mixed_grad = to_heads(outer_cols(grad_first_half, o_proj).astype(HALF), seq_count)
    query_grad, key_grad, value_grad = lax.map(
        back_recompute, (query_heads, key_heads, value_heads, valid, log_total, mixed_grad)
    )
    query_grad = from_heads(query_grad)
    key_grad = from_heads(key_grad)
    value_grad = from_heads(value_grad)
    q_bias_grad = jnp.sum(query_grad.astype(SINGLE), 0)
    v_bias_grad = jnp.sum(value_grad.astype(SINGLE), 0)
    q_grad = inner_rows(tokens, query_grad)
    k_grad = inner_rows(tokens, key_grad)
    v_grad = inner_rows(tokens, value_grad)
    input_part = (
        outer_cols(query_grad, q_proj)
        + outer_cols(key_grad, k_proj)
        + outer_cols(value_grad, v_proj)
    )
    tokens_grad = (
        grad_first + lax.psum(input_part.astype(jnp.bfloat16), "tensor").astype(jnp.float32)
    ).astype(HALF)
    q_summed, k_summed, v_summed, o_summed, up_summed, down_summed = (
        lax.psum_scatter(q_grad, "batch", scatter_dimension=0, tiled=True),
        lax.psum_scatter(k_grad, "batch", scatter_dimension=0, tiled=True),
        lax.psum_scatter(v_grad, "batch", scatter_dimension=0, tiled=True),
        lax.psum_scatter(o_grad, "batch", scatter_dimension=1, tiled=True),
        lax.psum_scatter(up_grad, "batch", scatter_dimension=0, tiled=True),
        lax.psum_scatter(down_grad, "batch", scatter_dimension=1, tiled=True),
    )
    small = lax.psum(
        (
            q_bias_grad,
            v_bias_grad,
            o_bias_grad,
            up_bias_grad,
            down_bias_grad,
            gain_first_grad,
            shift_first_grad,
            gain_second_grad,
            shift_second_grad,
        ),
        "batch",
    )
    return (
        output.astype(HALF),
        tokens_grad,
        q_summed,
        k_summed,
        v_summed,
        o_summed,
        up_summed,
        down_summed,
        small[0],
        small[1],
        small[2],
        small[3],
        small[4],
        small[5],
        small[6],
        small[7],
        small[8],
    )


def solution(mesh):
    in_specs = (
        P("batch", None),
        P("batch"),
        P("batch", "tensor"),
        P("batch", "tensor"),
        P("batch", "tensor"),
        P("tensor", "batch"),
        P("batch", "tensor"),
        P("tensor", "batch"),
        P("tensor"),
        P("tensor"),
        P(),
        P("tensor"),
        P(),
        P(),
        P(),
        P(),
        P(),
        P("batch", None),
    )
    out_specs = (
        P("batch", None),
        P("batch", None),
        P("batch", "tensor"),
        P("batch", "tensor"),
        P("batch", "tensor"),
        P("tensor", "batch"),
        P("batch", "tensor"),
        P("tensor", "batch"),
        P("tensor"),
        P("tensor"),
        P(),
        P("tensor"),
        P(),
        P(),
        P(),
        P(),
        P(),
    )
    return jax.shard_map(
        per_device, mesh=mesh, in_specs=in_specs, out_specs=out_specs, check_vma=False
    )
```

profile of v0, /device:TPU:0, one launch (start us, length us, event | category | flops | bytes accessed | tf_op | source)
XLA Modules:
  0.0 1401.5 jit_solution(4875458806947740931)
XLA Ops:
  12.4 48.5 %all_gather.21 = bf16[384,768]{0,1:T(8,128)(2,1)} all-gather(bf16[384,48]{0,1:T(8,128)(2,1)S(1)} %convert_element_type.129), channel_id=1, replica_groups=mesh['batch'=16,'tensor'=2] {'batch'}, dimensions={1}, use_global_device_ids=true | all-gather | bytes 626688 | tf_op jit(solution)/shard_map/all_gather | solution.py:134
  60.9 41.1 %all_gather.20 = bf16[768,384]{1,0:T(8,128)(2,1)} all-gather(bf16[48,384]{1,0:T(8,128)(2,1)S(1)} %convert_element_type.124), channel_id=1, replica_groups=mesh['batch'=16,'tensor'=2] {'batch'}, dimensions={0}, use_global_device_ids=true | all-gather | bytes 626688 | tf_op jit(solution)/shard_map/all_gather | solution.py:133
  102.0 43.7 %all_gather.19 = bf16[768,384]{1,0:T(8,128)(2,1)} all-gather(bf16[48,384]{1,0:T(8,128)(2,1)S(1)} %convert_element_type.122), channel_id=1, replica_groups=mesh['batch'=16,'tensor'=2] {'batch'}, dimensions={0}, use_global_device_ids=true | all-gather | bytes 626688 | tf_op jit(solution)/shard_map/all_gather | solution.py:132
  145.7 38.6 %all_gather.18 = bf16[768,384]{1,0:T(8,128)(2,1)S(1)} all-gather(bf16[48,384]{1,0:T(8,128)(2,1)S(1)} %convert_element_type.120), channel_id=1, replica_groups=mesh['batch'=16,'tensor'=2] {'batch'}, dimensions={0}, use_global_device_ids=true | all-gather | bytes 626688 | tf_op jit(solution)/shard_map/all_gather | solution.py:131
  226.4 32.4 %while.26 = (s32[]{:T(128)}, bf16[4,6,512,64]{2,3,1,0:T(8,128)(2,1)}, f32[4,6,512,1]{2,1,3,0:T(8,128)S(1)}, pred[4,512]{1,0:T(4,128)(4,1)S(1)}, bf16[4,6,512,64]...) while((s32[]{:T(128)}, ...), condition=%wide.region_3.4_spmd, body=%wide.region_0.3_spmd.sunk | while | flops 421524480 | bytes 33546908 | solution.py:149
  269.2 18.5 %all-reduce.6.cloned.1.call-done = bf16[2048,768]{1,0:T(8,128)(2,1)} async-done(((bf16[2048,768]{1,0:T(8,128)(2,1)}), bf16[2048,768]{1,0:T(8,128)(2,1)}) %all-reduce.6.cloned.1.call-update) | async-done | bytes 3145744 | tf_op jit(solution)/shard_map/psum | solution.py:151
  292.7 38.5 %all-gather.3.cloned.1.call-done = bf16[768,1536]{1,0:T(8,128)(2,1)} async-done(((bf16[48,1536]{1,0:T(8,128)(2,1)}), bf16[768,1536]{1,0:T(8,128)(2,1)}) %all-gather.3.cloned.1.call-update) | async-done | bytes 2359312 | tf_op jit(solution)/shard_map/all_gather | solution.py:135
  331.2 11.5 multiply_convert_fusion.1
  342.7 52.9 %all-gather.5.cloned.1.call-done = bf16[1536,768]{0,1:T(8,128)(2,1)} async-done(((bf16[1536,48]{0,1:T(8,128)(2,1)}), bf16[1536,768]{0,1:T(8,128)(2,1)}) %all-gather.5.cloned.1.call-update) | async-done | bytes 2359312 | tf_op jit(solution)/shard_map/all_gather | solution.py:136
  395.6 9.0 convolution_convert_fusion.2
  404.8 21.6 %all-reduce.8.cloned.1.call-done = bf16[2048,768]{1,0:T(8,128)(2,1)} async-done(((bf16[2048,768]{1,0:T(8,128)(2,1)}), bf16[2048,768]{1,0:T(8,128)(2,1)}) %all-reduce.8.cloned.1.call-update) | async-done | bytes 3145744 | tf_op jit(solution)/shard_map/psum | solution.py:161
  441.0 13.6 convert_reduce_fusion
  457.3 6.4 convolution_convert_fusion.1
  463.8 24.4 %all-reduce.10.cloned.1.call-done = bf16[2048,768]{1,0:T(8,128)(2,1)} async-done(((bf16[2048,768]{1,0:T(8,128)(2,1)}), bf16[2048,768]{1,0:T(8,128)(2,1)}) %all-reduce.10.cloned.1.call-update) | async-done | bytes 3145744 | tf_op jit(solution)/shard_map/psum | solution.py:176
  488.2 9.1 multiply_reduce_fusion.1
  518.3 61.2 %while.27 = (s32[]{:T(128)}, bf16[4,6,512,64]{2,3,1,0:T(8,128)(2,1)}, bf16[4,6,512,64]{2,3,1,0:T(8,128)(2,1)}, bf16[4,6,512,64]{2,3,1,0:T(8,128)(2,1)}, pred[4,5...) while((s32[]{:T(128)}, ...), condition=%wide.region_17.18_spmd, body=%wide.region_15.17_spmd.sunk | while | flops 1031205888 | bytes 57511576 | solution.py:186
  620.6 10.6 fusion.76
  631.5 11.6 fusion.79
  645.4 77.6 %all-reduce = (f32[384]{0:T(512)}, f32[384]{0:T(512)}, f32[768]{0:T(1024)}, f32[1536]{0:T(1024)}, f32[768]{0:T(1024)}, /*index=5*/f32[768]{0:T(1024)}, f32[768]{0:T(1024)}, f32[768]{0:T(1024)}, f32[768]{0:T(1024)}) all-reduce(f32[384]{0:T(512)S(1)} %reduce_sum.184, ...), channel_id=1, replica_groups=mesh['batch'=16,'tensor'=2] {'batch'}, use_global_device_ids=true, to_apply=%region_26.27 | all-reduce | flops 6912 | bytes 55296 | tf_op jit(solution)/shard_map/psum | solution.py:213
  729.1 124.0 %reduce-scatter.21.cloned.1.call-done = f32[48,384]{1,0:T(8,128)} async-done(((f32[768,384]{1,0:T(8,128)}), f32[48,384]{1,0:T(8,128)}) %reduce-scatter.21.cloned.1.call-update) | async-done | bytes 73744
  853.1 128.1 %reduce-scatter.19.cloned.1.call-done = f32[48,384]{1,0:T(8,128)} async-done(((f32[768,384]{1,0:T(8,128)}), f32[48,384]{1,0:T(8,128)}) %reduce-scatter.19.cloned.1.call-update) | async-done | bytes 73744
  981.2 128.1 %reduce-scatter.23.cloned.1.call-done = f32[48,384]{1,0:T(8,128)} async-done(((f32[768,384]{1,0:T(8,128)}), f32[48,384]{1,0:T(8,128)}) %reduce-scatter.23.cloned.1.call-update) | async-done | bytes 73744
  1109.3 142.2 %reduce-scatter.17.cloned.1.call-done = f32[1536,48]{0,1:T(8,128)} async-done(((f32[1536,768]{0,1:T(8,128)}), f32[1536,48]{0,1:T(8,128)}) %reduce-scatter.17.cloned.1.call-update) | async-done | bytes 294928 | tf_op jit(solution)/shard_map/reduce_scatter | solution.py:211
  1251.5 142.6 %reduce-scatter.15.cloned.1.call-done = f32[48,1536]{1,0:T(8,128)} async-done(((f32[768,1536]{1,0:T(8,128)}), f32[48,1536]{1,0:T(8,128)}) %reduce-scatter.15.cloned.1.call-update) | async-done | bytes 294928 | tf_op jit(solution)/shard_map/reduce_scatter | solution.py:210
  (240 shorter events, 242.1 us)
Async XLA Ops:
  8.0 279.7 %all-reduce.6.cloned.1.call-start = ((), (), s32[]{:S(2)}) async-start(), calls=%async_computation.6 | async-start | bytes 6291456 | tf_op jit(solution)/shard_map/psum | solution.py:151
  190.1 9.6 copy-start.1
  203.7 9.3 copy-start.37
  263.1 24.6 %copy-start.24 = (f32[768]{0:T(1024)S(1)}, f32[768]{0:T(1024)}, u32[]{:S(2)}) copy-start(f32[768]{0:T(1024)} %param.32) | copy-start | bytes 9220
  266.6 64.5 %all-gather.3.cloned.1.call-start = ((), (), s32[]{:S(2)}) async-start(), calls=%async_computation.7 | async-start | bytes 2506752 | tf_op jit(solution)/shard_map/all_gather | solution.py:135
  267.4 128.2 %all-gather.5.cloned.1.call-start = ((), (), s32[]{:S(2)}) async-start(), calls=%async_computation.8 | async-start | bytes 2506752 | tf_op jit(solution)/shard_map/all_gather | solution.py:136
  269.1 62.1 %copy-start.25 = (f32[768]{0:T(1024)S(1)}, f32[768]{0:T(1024)}, u32[]{:S(2)}) copy-start(f32[768]{0:T(1024)} %param.35) | copy-start | bytes 9220
  269.1 62.1 %copy-start.32 = (f32[768]{0:T(1024)S(1)}, f32[768]{0:T(1024)}, u32[]{:S(2)}) copy-start(f32[768]{0:T(1024)} %param.36) | copy-start | bytes 9220
  269.1 62.0 %copy-start.36 = (f32[1536]{0:T(1024)S(1)}, f32[1536]{0:T(1024)}, u32[]{:S(2)}) copy-start(f32[1536]{0:T(1024)} %param.33) | copy-start | bytes 18436
  269.2 157.2 %all-reduce.8.cloned.1.call-start = ((), (), s32[]{:S(2)}) async-start(), calls=%async_computation.9 | async-start | bytes 6291456 | tf_op jit(solution)/shard_map/psum | solution.py:161
  395.6 30.7 %copy-start.30 = (f32[768]{0:T(1024)S(1)}, f32[768]{0:T(1024)}, u32[]{:S(2)}) copy-start(f32[768]{0:T(1024)} %param.34) | copy-start | bytes 9220
  404.7 83.5 %all-reduce.10.cloned.1.call-start = ((), (), s32[]{:S(2)}) async-start(), calls=%async_computation.10 | async-start | bytes 6291456 | tf_op jit(solution)/shard_map/psum | solution.py:176
  441.0 13.7 copy-start.4
  441.0 16.3 %copy-start.34 = (bf16[768,1536]{1,0:T(8,128)(2,1)S(1)}, bf16[768,1536]{1,0:T(8,128)(2,1)}, u32[]{:S(2)}) copy-start(bf16[768,1536]{1,0:T(8,128)(2,1)} %all-gather.3.cloned.1.call-done) | copy-start | bytes 7077892
  463.7 259.3 %all-reduce.12.cloned.1.call-start = ((), (), s32[]{:S(2)}) async-start(), calls=%async_computation.11 | async-start | bytes 6291456 | tf_op jit(solution)/shard_map/psum | solution.py:203
  488.2 9.2 copy-start.3
  488.2 9.2 copy-start.6
  593.6 135.5 %reduce-scatter.13.cloned.1.call-start = ((), (), s32[]{:S(2)}) async-start(), calls=%async_computation.12 | async-start | bytes 1253376 | tf_op jit(solution)/shard_map/reduce_scatter | solution.py:209
  600.1 253.1 %reduce-scatter.21.cloned.1.call-start = ((), (), s32[]{:S(2)}) async-start(), calls=%async_computation.16 | async-start | bytes 1253376
  607.1 374.1 %reduce-scatter.19.cloned.1.call-start = ((), (), s32[]{:S(2)}) async-start(), calls=%async_computation.15 | async-start | bytes 1253376
  613.8 495.5 %reduce-scatter.23.cloned.1.call-start = ((), (), s32[]{:S(2)}) async-start(), calls=%async_computation.17 | async-start | bytes 1253376
  620.5 11.0 copy-start.33
  620.5 631.0 %reduce-scatter.17.cloned.1.call-start = ((), (), s32[]{:S(2)}) async-start(), calls=%async_computation.14 | async-start | bytes 5013504 | tf_op jit(solution)/shard_map/reduce_scatter | solution.py:211
  631.2 762.9 %reduce-scatter.15.cloned.1.call-start = ((), (), s32[]{:S(2)}) async-start(), calls=%async_computation.13 | async-start | bytes 5013504 | tf_op jit(solution)/shard_map/reduce_scatter | solution.py:210
  (36 other events, 106.2 us)
Sparse Core Ops, SparseCore 0:
  266.8 20.9 all-reduce.5
  404.8 21.4 all-reduce.7
  463.8 24.3 all-reduce.9
  593.7 24.3 all-reduce.11
Sparse Core Ops, SparseCore 1:
  270.9 60.3 all-gather.2
  334.8 60.8 all-gather.4
  600.1 124.8 reduce-scatter.12
  730.3 122.7 reduce-scatter.20
  858.5 122.7 reduce-scatter.18
  986.6 122.7 reduce-scatter.22
  1114.9 136.5 reduce-scatter.16
  1257.9 136.1 reduce-scatter.14
where the time goes:
time: 1410 us; the launch traced here: 1400 us
  waiting for transfers between devices  821 us (58%)
  blocking collectives  250 us (18%)
  matrix products  181 us (13%)
  local copies, waits for them, and re-layouts  68.8 us (5%)
  other arithmetic  62.4 us (4%)
  between operations  16.1 us (1%)
    unnamed x15, waiting for transfers between devices  380 us
    reduce_scatter x1, waiting for transfers between devices, per_device(): lax.psum_scatter(up_grad, 'batch', scatter_dimension=0, tiled=True)  143 us
    reduce_scatter x1, waiting for transfers between devices, per_device(): lax.psum_scatter(down_grad, 'batch', scatter_dimension=1, tiled=True)  142 us
    psum x1, blocking collectives, per_device(): lax.psum((q_bias_grad, v_bias_grad, o_bias_grad, up_bias_grad, down_bias_...  77.6 us
    all_gather x1, waiting for transfers between devices, per_device(): lax.all_gather(down_projection_weight.astype(HALF), 'batch', axis=1, tile...  52.9 us
    all_gather x1, blocking collectives, per_device(): lax.all_gather(output_weight.astype(HALF), 'batch', axis=1, tiled=True)  48.5 us
    all_gather x1, blocking collectives, per_device(): lax.all_gather(k_weight.astype(HALF), 'batch', axis=0, tiled=True)  43.7 us
    all_gather x1, blocking collectives, per_device(): lax.all_gather(v_weight.astype(HALF), 'batch', axis=0, tiled=True)  41.1 us
  transfers between devices with their start and end apart: 12, of which 10 were waited for; matrix products, arithmetic and copies ran while one was open for 5% of the time, Pallas kernels for 0%

commit v1 on v0

v1 whole, which is shorter than its diff:
```python
import functools
import math

import jax
import jax.numpy as jnp
from jax import lax
from jax.experimental import pallas as pl
from jax.experimental.pallas import tpu as pltpu
from jax.sharding import PartitionSpec as P

HEAD_DIM = 64
LANES = 128
EPSILON = 1e-12
NEGATIVE = -1000000000.0
HALF = jnp.bfloat16
SINGLE = jnp.float32
SWAP = ((0, 1), (1, 0))


def matmul(left, right):
    return jnp.dot(left, right, preferred_element_type=SINGLE)


def inner_rows(left, right):
    return lax.dot_general(left, right, (((0,), (0,)), ((), ())), preferred_element_type=SINGLE)


def outer_cols(left, right):
    return lax.dot_general(left, right, (((1,), (1,)), ((), ())), preferred_element_type=SINGLE)


def layer_norm(values, gain, shift):
    center = values - jnp.mean(values, -1, keepdims=True)
    inverse = lax.rsqrt(jnp.mean(center * center, -1, keepdims=True) + EPSILON)
    normal = center * inverse
    return (normal * gain + shift, normal, inverse)


def norm_back(grad, normal, inverse, gain):
    scaled = grad * gain
    inner = (
        scaled
        - jnp.mean(scaled, -1, keepdims=True)
        - normal * jnp.mean(scaled * normal, -1, keepdims=True)
    )
    return inner * inverse


def gelu_parts(upper):
    cdf = 0.5 * (1.0 + lax.erf(upper * (1.0 / math.sqrt(2.0))))
    density = jnp.exp(-0.5 * upper * upper) * (1.0 / math.sqrt(2.0 * math.pi))
    return (upper * cdf, cdf + upper * density)


def head_sides():
    lane = lax.broadcasted_iota(jnp.int32, (1, LANES), 1)
    first = (lane < HEAD_DIM).astype(SINGLE)
    return (first.astype(HALF), (1.0 - first).astype(HALF))


def attend_kernel(len_ref, tok_ref, w_ref, b_ref, qkv_ref, mixed_ref, lse_ref):
    span = tok_ref.shape[0]
    width = mixed_ref.shape[1]
    length = len_ref[pl.program_id(0)]
    qkv_ref[...] = (matmul(tok_ref[...], w_ref[...]) + b_ref[...]).astype(HALF)
    sides = head_sides()
    keep = lax.broadcasted_iota(jnp.int32, (span, span), 0) < length
    for pair in range(width // LANES):
        at = LANES * pair
        query = qkv_ref[:, pl.ds(at, LANES)] * HALF(HEAD_DIM**-0.5)
        keys = qkv_ref[:, pl.ds(width + at, LANES)]
        values = qkv_ref[:, pl.ds(2 * width + at, LANES)]
        mixed = 0.0
        for h in range(2):
            scores = jnp.where(keep, outer_cols(keys * sides[h], query), NEGATIVE)
            top = jnp.max(scores, 0, keepdims=True)
            expo = jnp.exp(scores - top)
            total = jnp.sum(expo, 0, keepdims=True)
            lse_ref[0, 2 * pair + h : 2 * pair + h + 1, :] = top + jnp.log(total)
            mixed += inner_rows(values * sides[h], expo.astype(HALF)) * (1.0 / total)
        mixed_ref[:, pl.ds(at, LANES)] = mixed.T.astype(HALF)


def attend(lengths, tokens, weight, bias):
    rows, depth = tokens.shape
    seqs = lengths.shape[0]
    span = rows // seqs
    width = weight.shape[1] // 3
    heads = width // HEAD_DIM
    return pl.pallas_call(
        attend_kernel,
        grid_spec=pltpu.PrefetchScalarGridSpec(
            num_scalar_prefetch=1,
            grid=(seqs,),
            in_specs=[
                pl.BlockSpec((span, depth), lambda i, n: (i, 0)),
                pl.BlockSpec((depth, 3 * width), lambda i, n: (0, 0)),
                pl.BlockSpec((1, 3 * width), lambda i, n: (0, 0)),
            ],
            out_specs=[
                pl.BlockSpec((span, 3 * width), lambda i, n: (i, 0)),
                pl.BlockSpec((span, width), lambda i, n: (i, 0)),
                pl.BlockSpec((1, heads, span), lambda i, n: (i, 0, 0)),
            ],
        ),
        out_shape=[
            jax.ShapeDtypeStruct((rows, 3 * width), HALF),
            jax.ShapeDtypeStruct((rows, width), HALF),
            jax.ShapeDtypeStruct((seqs, heads, span), SINGLE),
        ],
        compiler_params=pltpu.CompilerParams(vmem_limit_bytes=40 << 20),
        cost_estimate=pl.CostEstimate(
            flops=30_000_000_000, bytes_accessed=8_000_000, transcendentals=0
        ),
        name="attend",
    )(lengths, tokens, weight, bias)


def attend_back_kernel(len_ref, qkv_ref, lse_ref, grad_ref, out_ref, bias_ref):
    span, width = grad_ref.shape
    step = pl.program_id(0)
    length = len_ref[step]
    sides = head_sides()
    keep = lax.broadcasted_iota(jnp.int32, (span, span), 0) < length

    @pl.when(step == 0)
    def _():
        bias_ref[...] = jnp.zeros_like(bias_ref)

    for pair in range(width // LANES):
        at = LANES * pair
        query = qkv_ref[:, pl.ds(at, LANES)] * HALF(HEAD_DIM**-0.5)
        keys = qkv_ref[:, pl.ds(width + at, LANES)]
        values = qkv_ref[:, pl.ds(2 * width + at, LANES)]
        grad = grad_ref[:, pl.ds(at, LANES)]
        query_grad = key_grad = value_grad = 0.0
        for h in range(2):
            side_keys = keys * sides[h]
            scores = jnp.where(keep, outer_cols(side_keys, query), NEGATIVE)
            probs = jnp.exp(scores - lse_ref[0, 2 * pair + h : 2 * pair + h + 1, :])
            value_grad += matmul(probs.astype(HALF), grad * sides[h])
            prob_grad = outer_cols(values * sides[h], grad)
            delta = jnp.sum(probs * prob_grad, 0, keepdims=True)
            score_grad = (probs * (prob_grad - delta)).astype(HALF)
            key_grad += matmul(score_grad, query * sides[h])
            query_grad += inner_rows(side_keys, score_grad)
        query_grad = (query_grad * HEAD_DIM**-0.5).T
        for j, grads in enumerate((query_grad, key_grad, value_grad)):
            out_ref[:, pl.ds(j * width + at, LANES)] = grads.astype(HALF)
            if j != 1:
                bias_ref[:, pl.ds(j * width + at, LANES)] += jnp.sum(grads, 0, keepdims=True)


def attend_back(lengths, qkv, lse, grad):
    rows, width = grad.shape
    seqs = lengths.shape[0]
    span = rows // seqs
    heads = width // HEAD_DIM
    return pl.pallas_call(
        attend_back_kernel,
        grid_spec=pltpu.PrefetchScalarGridSpec(
            num_scalar_prefetch=1,
            grid=(seqs,),
            in_specs=[
                pl.BlockSpec((span, 3 * width), lambda i, n: (i, 0)),
                pl.BlockSpec((1, heads, span), lambda i, n: (i, 0, 0)),
                pl.BlockSpec((span, width), lambda i, n: (i, 0)),
            ],
            out_specs=[
                pl.BlockSpec((span, 3 * width), lambda i, n: (i, 0)),
                pl.BlockSpec((1, 3 * width), lambda i, n: (0, 0)),
            ],
        ),
        out_shape=[
            jax.ShapeDtypeStruct((rows, 3 * width), HALF),
            jax.ShapeDtypeStruct((1, 3 * width), SINGLE),
        ],
        compiler_params=pltpu.CompilerParams(vmem_limit_bytes=40 << 20),
        cost_estimate=pl.CostEstimate(
            flops=32_000_000_000, bytes_accessed=8_000_000, transcendentals=0
        ),
        name="attend_back",
    )(lengths, qkv, lse, grad)


def middle_kernel(
    chunk,
    mix_a,
    mix_b,
    tok_ref,
    cot_ref,
    o_a,
    o_b,
    up_a,
    up_b,
    down_a,
    down_b,
    up_bias,
    vec_ref,
    out_ref,
    act_a,
    act_b,
    ugrad_a,
    ugrad_b,
    normed_ref,
    second_ref,
    first_ref,
    first_half_ref,
    mgrad_a,
    mgrad_b,
    vec_grad,
    up_bias_grad,
    slope_ref,
):
    @pl.when(pl.program_id(0) == 0)
    def _():
        vec_grad[...] = jnp.zeros_like(vec_grad)
        up_bias_grad[...] = jnp.zeros_like(up_bias_grad)

    o_bias, down_bias, gain_1, shift_1, gain_2, shift_2 = (
        vec_ref[j : j + 1, :] for j in range(6)
    )
    attention = outer_cols(mix_a[...], o_a[...]) + outer_cols(mix_b[...], o_b[...])
    normed, normal_1, inverse_1 = layer_norm(
        tok_ref[...].astype(SINGLE) + attention + o_bias, gain_1, shift_1
    )
    normed_half = normed.astype(HALF)
    normed_ref[...] = normed_half
    units = up_a.shape[1]
    branch = 0.0
    for half, (up, down, act) in enumerate(((up_a, down_a, act_a), (up_b, down_b, act_b))):
        for c in range(units // chunk):
            here = pl.ds(c * chunk, chunk)
            there = pl.ds(half * units + c * chunk, chunk)
            active, slope = gelu_parts(matmul(normed_half, up[:, here]) + up_bias[:, there])
            active = active.astype(HALF)
            act[:, here] = active
            slope_ref[:, there] = slope
            branch += outer_cols(active, down[:, here])
    output, normal_2, inverse_2 = layer_norm(normed + branch + down_bias, gain_2, shift_2)
    out_ref[...] = output.astype(HALF)
    cot = cot_ref[...].astype(SINGLE)
    second = norm_back(cot, normal_2, inverse_2, gain_2)
    second_half = second.astype(HALF)
    second_ref[...] = second_half
    normed_grad = second
    for half, (up, down, ugrad) in enumerate(((up_a, down_a, ugrad_a), (up_b, down_b, ugrad_b))):
        for c in range(units // chunk):
            here = pl.ds(c * chunk, chunk)
            there = pl.ds(half * units + c * chunk, chunk)
            upper_grad = matmul(second_half, down[:, here]) * slope_ref[:, there]
            up_bias_grad[:, there] += jnp.sum(upper_grad, 0, keepdims=True)
            upper_grad = upper_grad.astype(HALF)
            ugrad[:, here] = upper_grad
            normed_grad += outer_cols(upper_grad, up[:, here])
    first = norm_back(normed_grad, normal_1, inverse_1, gain_1)
    first_ref[...] = first
    first_half = first.astype(HALF)
    first_half_ref[...] = first_half
    mgrad_a[...] = matmul(first_half, o_a[...]).astype(HALF)
    mgrad_b[...] = matmul(first_half, o_b[...]).astype(HALF)
    sums = (first, second, normed_grad * normal_1, normed_grad, cot * normal_2, cot)
    for j, rows in enumerate(sums):
        vec_grad[j : j + 1, :] += jnp.sum(rows, 0, keepdims=True)


def middle(mixes, tokens, cotangent, o_halves, up_halves, down_halves, up_bias, vectors):
    rows, depth = tokens.shape
    width = mixes[0].shape[1]
    units = up_halves[0].shape[1]
    block = math.gcd(rows, 256)
    chunk = math.gcd(units, 768)
    wide = lambda columns: pl.BlockSpec((block, columns), lambda i: (i, 0))
    held = lambda a: pl.BlockSpec(a.shape, lambda i: (0, 0), pipeline_mode=pl.Buffered(1))
    kept = (*o_halves, *up_halves, *down_halves, up_bias, vectors)
    shape = jax.ShapeDtypeStruct
    return pl.pallas_call(
        functools.partial(middle_kernel, chunk),
        grid=(rows // block,),
        in_specs=[wide(width), wide(width), wide(depth), wide(depth)] + [held(a) for a in kept],
        out_specs=[wide(depth)]
        + [wide(units)] * 4
        + [wide(depth)] * 4
        + [wide(width)] * 2
        + [
            pl.BlockSpec((8, depth), lambda i: (0, 0)),
            pl.BlockSpec((1, 2 * units), lambda i: (0, 0)),
        ],
        out_shape=[shape((rows, depth), HALF)]
        + [shape((rows, units), HALF)] * 4
        + [shape((rows, depth), HALF)] * 2
        + [shape((rows, depth), SINGLE), shape((rows, depth), HALF)]
        + [shape((rows, width), HALF)] * 2
        + [shape((8, depth), SINGLE), shape((1, 2 * units), SINGLE)],
        scratch_shapes=[pltpu.VMEM((block, 2 * units), SINGLE)],
        compiler_params=pltpu.CompilerParams(vmem_limit_bytes=58 << 20),
        cost_estimate=pl.CostEstimate(
            flops=60_000_000_000, bytes_accessed=40_000_000, transcendentals=0
        ),
        name="middle",
    )(*mixes, tokens, cotangent, *kept)


def swap(array):
    return lax.ppermute(array, "tensor", SWAP)


def hop(array, distance, size):
    return lax.ppermute(array, "batch", [(i, i ^ distance) for i in range(size)])


def place_kernel(distances, me_ref, *refs):
    count = len(distances)
    blocks, outs, sems = refs[:count], refs[count:-1], refs[-1]
    rows = blocks[0].shape[0]
    copies = []
    for j, distance in enumerate(distances):
        at = pl.multiple_of((me_ref[0] ^ distance) * rows, rows)
        left = 0
        for n, out in enumerate(outs):
            columns = out.shape[1]
            copies.append(
                pltpu.make_async_copy(
                    blocks[j].at[:, pl.ds(left, columns)],
                    out.at[pl.ds(at, rows), :],
                    sems.at[j, n],
                )
            )
            left += columns
    for copy in copies:
        copy.start()
    for copy in copies:
        copy.wait()


def place(me, blocks, widths):
    distances = sorted(blocks)
    rows = blocks[0].shape[0]
    return pl.pallas_call(
        functools.partial(place_kernel, distances),
        grid_spec=pltpu.PrefetchScalarGridSpec(
            num_scalar_prefetch=1,
            grid=(1,),
            in_specs=[pl.BlockSpec(memory_space=pl.ANY)] * len(distances),
            out_specs=[pl.BlockSpec(memory_space=pl.ANY)] * len(widths),
            scratch_shapes=[pltpu.SemaphoreType.DMA((len(distances), len(widths)))],
        ),
        out_shape=[
            jax.ShapeDtypeStruct((len(distances) * rows, columns), HALF) for columns in widths
        ],
        compiler_params=pltpu.CompilerParams(vmem_limit_bytes=4 << 20),
        name="place",
    )(me.reshape(1), *[blocks[d] for d in distances])


def gather(me, size, part, widths):
    if size != 16:
        whole = lax.all_gather(part, "batch", axis=0, tiled=True)
        edges = [sum(widths[:n]) for n in range(1, len(widths))]
        return jnp.split(whole, edges, axis=1)
    blocks = {0: part}
    for z in (4, 8, 12):
        blocks[z] = hop(part, z, size)
    for z in (0, 4, 8, 12):
        blocks[z + 1] = hop(blocks[z], 1, size)
        blocks[z + 2] = hop(blocks[z], 2, size)
    for z in (0, 4):
        blocks[z + 3] = hop(blocks[z + 2], 1, size)
    for z in (8, 12):
        blocks[z + 3] = hop(blocks[z + 1], 2, size)
    return place(me, blocks, widths)


def scatter(me, size, whole):
    if size != 16:
        return lax.psum_scatter(whole.astype(SINGLE), "batch", scatter_dimension=0, tiled=True)
    x, y, z = me & 1, (me >> 1) & 1, me >> 2
    rows, columns = whole.shape
    whole = whole.reshape(4, 2, 2, rows // 16, columns)
    pick = lambda array, at, axis: lax.dynamic_index_in_dim(array, at, axis, keepdims=False)
    low, high = whole[:2], whole[2:]
    low_in = hop(pick(low, 1 - x, 2), 1, size)
    high_in = hop(pick(high, 1 - y, 1), 2, size)
    low = pick(low, x, 2) + low_in
    high = pick(high, y, 1) + high_in
    low_in = hop(pick(low, 1 - y, 1), 2, size)
    high_in = hop(pick(high, 1 - x, 1), 1, size)
    column = jnp.concatenate([pick(low, y, 1) + low_in, pick(high, x, 1) + high_in])
    total = pick(column, z, 0).astype(SINGLE)
    for d in (1, 2, 3):
        total += hop(pick(column, z ^ d, 0), 4 * d, size).astype(SINGLE)
    return total


def total_over_batch(size, vector):
    if size != 16:
        return lax.psum(vector, "batch")
    for d in (1, 2, 4, 8):
        vector = vector + hop(vector, d, size)
    return vector


def weight_grad(left, right_own, right_other):
    received = swap(inner_rows(left, right_other).astype(HALF))
    return (inner_rows(left, right_own) + received.astype(SINGLE)).astype(HALF)


def per_device(
    size,
    tokens,
    lengths,
    q_weight,
    k_weight,
    v_weight,
    output_weight,
    up_weight,
    down_projection_weight,
    q_bias,
    v_bias,
    o_bias,
    up_bias,
    down_bias,
    gain_first,
    shift_first,
    gain_second,
    shift_second,
    out_grad,
):
    me = lax.axis_index("batch")
    core = lax.axis_index("tensor")
    depth = tokens.shape[1]
    width = q_weight.shape[1]
    units = up_weight.shape[1]
    rows = tokens.shape[0] // 2
    seqs = lengths.shape[0] // 2

    qkv_part = jnp.concatenate([w.astype(HALF) for w in (q_weight, k_weight, v_weight)], 1)
    up_part = jnp.concatenate([output_weight.astype(HALF).T, up_weight.astype(HALF)], 1)
    down_part = down_projection_weight.astype(HALF).T
    tokens = lax.dynamic_slice_in_dim(tokens, core * rows, rows)
    cotangent = lax.dynamic_slice_in_dim(out_grad, core * rows, rows)
    lengths = lax.dynamic_slice_in_dim(lengths, core * seqs, seqs)
    biases = jnp.concatenate([q_bias, jnp.zeros_like(q_bias), v_bias, up_bias])
    other_biases = swap(biases)
    qkv_bias = [b[: 3 * width].reshape(1, -1) for b in (biases, other_biases)]
    up_biases = jnp.concatenate([b[3 * width :] for b in (biases, other_biases)]).reshape(1, -1)
    blank = jnp.zeros_like(o_bias)
    vectors = jnp.stack(
        [o_bias, down_bias, gain_first, shift_first, gain_second, shift_second, blank, blank]
    )

    (qkv_own,) = gather(me, size, qkv_part, (3 * width,))
    o_own, up_own = gather(me, size, up_part, (width, units))
    (down_own,) = gather(me, size, down_part, (units,))
    qkv_w = (qkv_own, swap(qkv_own))
    o_w = (o_own, swap(o_own))
    up_w = (up_own, swap(up_own))
    down_w = (down_own, swap(down_own))

    fronts = [attend(lengths, tokens, w, b) for w, b in zip(qkv_w, qkv_bias)]
    mixes = [front[1] for front in fronts]
    (
        output,
        act_own,
        act_other,
        ugrad_own,
        ugrad_other,
        normed,
        second,
        first,
        first_half,
        mgrad_own,
        mgrad_other,
        vec_grad,
        up_bias_grad,
    ) = middle(mixes, tokens, cotangent, o_w, up_w, down_w, up_biases, vectors)

    down_grad = weight_grad(second, act_own, act_other)
    up_grad = weight_grad(normed, ugrad_own, ugrad_other)
    o_grad = weight_grad(first_half, mixes[0], mixes[1])
    down_sum = scatter(me, size, down_grad)
    up_sum = scatter(me, size, up_grad)
    o_sum = scatter(me, size, o_grad)

    back_other, bias_other = attend_back(lengths, fronts[1][0], fronts[1][2], mgrad_other)
    back_own, bias_own = attend_back(lengths, fronts[0][0], fronts[0][2], mgrad_own)
    qkv_grad = weight_grad(tokens, back_own, back_other)
    qkv_sum = scatter(me, size, qkv_grad)

    shared = vec_grad[:6].reshape(-1)
    mine = jnp.concatenate([bias_own[0], up_bias_grad[0, :units], shared])
    theirs = jnp.concatenate([bias_other[0], up_bias_grad[0, units:], shared])
    small = total_over_batch(size, mine + swap(theirs))

    tokens_grad = (
        first + outer_cols(back_own, qkv_w[0]) + outer_cols(back_other, qkv_w[1])
    ).astype(HALF)

    def both(part):
        other = swap(part)
        low = jnp.where(core == 0, part, other)
        high = jnp.where(core == 0, other, part)
        return jnp.concatenate([low, high])

    edge = 3 * width + units
    o_bias_grad, down_bias_grad, gain_1, shift_1, gain_2, shift_2 = jnp.split(small[edge:], 6)
    return (
        both(output),
        both(tokens_grad),
        qkv_sum[:, :width],
        qkv_sum[:, width : 2 * width],
        qkv_sum[:, 2 * width :],
        o_sum.T,
        up_sum,
        down_sum.T,
        small[:width],
        small[2 * width : 3 * width],
        o_bias_grad,
        small[3 * width : edge],
        down_bias_grad,
        gain_1,
        shift_1,
        gain_2,
        shift_2,
    )


def solution(mesh):
    in_specs = (
        P("batch", None),
        P("batch"),
        P("batch", "tensor"),
        P("batch", "tensor"),
        P("batch", "tensor"),
        P("tensor", "batch"),
        P("batch", "tensor"),
        P("tensor", "batch"),
        P("tensor"),
        P("tensor"),
        P(),
        P("tensor"),
        P(),
        P(),
        P(),
        P(),
        P(),
        P("batch", None),
    )
    out_specs = (
        P("batch", None),
        P("batch", None),
        P("batch", "tensor"),
        P("batch", "tensor"),
        P("batch", "tensor"),
        P("tensor", "batch"),
        P("batch", "tensor"),
        P("tensor", "batch"),
        P("tensor"),
        P("tensor"),
        P(),
        P("tensor"),
        P(),
        P(),
        P(),
        P(),
        P(),
    )
    return jax.shard_map(
        functools.partial(per_device, mesh.shape["batch"]),
        mesh=mesh,
        in_specs=in_specs,
        out_specs=out_specs,
        check_vma=False,
    )
```

time: 1410 us -> 338 us (0.24)
  waiting for transfers between devices: 821 us -> 80.1 us
  blocking collectives: 250 us -> 0 us
  matrix products: 181 us -> 25.3 us
  starting transfers between devices: 1.06 us -> 95.2 us
  Pallas kernels: 0 us -> 83.2 us
  other arithmetic: 62.4 us -> 15 us
  local copies, waits for them, and re-layouts: 68.8 us -> 33.1 us
    unnamed x15 -> x0, waiting for transfers between devices: 380 us -> none
    reduce_scatter x3 -> x0, waiting for transfers between devices: 285 us -> none  [the longest x1 143 us: per_device(): lax.psum_scatter(up_grad, 'batch', scatter_dimension=0, tiled=True)]
    all_gather x4 -> x0, blocking collectives: 172 us -> none  [the longest x1 48.5 us: per_device(): lax.all_gather(output_weight.astype(HALF), 'batch', axis=1, tiled=True)]
    dot_general x34 -> x0, matrix products: 111 us -> none  [the longest x6 36.9 us: matmul(): return jnp.dot(left, right, preferred_element_type=SINGLE)]
    ppermute x0 -> x89, starting transfers between devices: none -> 95.2 us  [the longest x77 93.1 us: hop(): lax.ppermute(array, 'batch', [(i, i ^ distance) for i in range(size)])]
    all_gather x2 -> x0, waiting for transfers between devices: 91.4 us -> none  [the longest x1 52.9 us: per_device(): lax.all_gather(down_projection_weight.astype(HALF), 'batch', axis=1, tile...]
    pallas_call x0 -> x8, Pallas kernels: none -> 83.2 us  [the longest x1 38.5 us: middle(): pl.pallas_call(functools.partial(middle_kernel, chunk), grid=(rows // blo...]
    ppermute x0 -> x89, waiting for transfers between devices: none -> 80.1 us  [the longest x77 79.9 us: hop(): lax.ppermute(array, 'batch', [(i, i ^ distance) for i in range(size)])]
  transfers between devices with their start and end apart: 12 -> 89, of which waited for: 10 -> 26; matrix products, arithmetic and copies ran while one was open for 5% -> 13% of each run, Pallas kernels for 0% -> 10%
where the time goes in v1:
time: 338 us; the launch traced here: 334 us
  starting transfers between devices  95.2 us (28%)
  Pallas kernels  83.2 us (25%)
  waiting for transfers between devices  80.1 us (24%)
  local copies, waits for them, and re-layouts  33.1 us (10%)
  matrix products  25.3 us (7%)
  other arithmetic  15 us (4%)
    ppermute x77, starting transfers between devices, hop(): lax.ppermute(array, 'batch', [(i, i ^ distance) for i in range(size)])  93.1 us
    ppermute x77, waiting for transfers between devices, hop(): lax.ppermute(array, 'batch', [(i, i ^ distance) for i in range(size)])  79.9 us
    pallas_call x1, Pallas kernels, middle(): pl.pallas_call(functools.partial(middle_kernel, chunk), grid=(rows // blo...  38.5 us
    unnamed x174, local copies, waits for them, and re-layouts  23.4 us
    dot_general x8, matrix products, inner_rows(): lax.dot_general(left, right, (((0,), (0,)), ((), ())), preferred_element_...  20.8 us
    pallas_call x2, Pallas kernels, attend_back(): pl.pallas_call(attend_back_kernel, grid_spec=pltpu.PrefetchScalarGridSpec...  20.3 us
    pallas_call x2, Pallas kernels, attend(): pl.pallas_call(attend_kernel, grid_spec=pltpu.PrefetchScalarGridSpec(num_...  16.8 us
    pallas_call x3, Pallas kernels, place(): pl.pallas_call(functools.partial(place_kernel, distances), grid_spec=pltp...  7.54 us
  transfers between devices with their start and end apart: 89, of which 26 were waited for; matrix products, arithmetic and copies ran while one was open for 13% of the time, Pallas kernels for 10%

profile of v1, /device:TPU:0, one launch (start us, length us, event | category | flops | bytes accessed | tf_op | source)
XLA Modules:
  0.0 334.1 jit_solution(15149304132209769254)
XLA Ops:
  3.5 4.1 %collective-permute-start.7 = (bf16[48,1152]{1,0:T(8,128)(2,1)S(1)}, bf16[48,1152]{1,0:T(8,128)(2,1)S(1)}, u32[]{:S(2)}, u32[]{:S(2)}) collective-permute-start(bf16[48,1152]{1,0:T(8,128)(2,1)S(1)} %pad_maximum_fusion.3.refs_0_), channel_id=1, source_target_pairs={{0,16},{2,18},{4,20},{6,22},{8,24},{10,26},{12,28},{14,30},{16,0},... | collective-permute-start | bytes 331784 | tf_op jit(solution)/shard_map/ppermute | solution.py:309
  24.9 7.1 %collective-permute-done.41.refs_8_ = bf16[48,1536]{1,0:T(8,128)(2,1)} collective-permute-done((bf16[48,1536]{1,0:T(8,128)(2,1)S(1)}, bf16[48,1536]{1,0:T(8,128)(2,1)}, u32[]{:S(2)}, u32[]{:S(2)}) %collective-permute-start.41) | collective-permute-done | bytes 147488 | tf_op jit(solution)/shard_map/ppermute | solution.py:309
  37.7 9.3 %collective-permute-done.24.refs_8_ = bf16[48,1920]{1,0:T(8,128)(2,1)} collective-permute-done((bf16[48,1920]{1,0:T(8,128)(2,1)S(1)}, bf16[48,1920]{1,0:T(8,128)(2,1)}, u32[]{:S(2)}, u32[]{:S(2)}) %collective-permute-start.24) | collective-permute-done | bytes 184352 | tf_op jit(solution)/shard_map/ppermute | solution.py:309
  77.0 3.5 %collective-permute-done.14.refs_15_ = bf16[48,1152]{1,0:T(8,128)(2,1)S(1)} collective-permute-done((bf16[48,1152]{1,0:T(8,128)(2,1)}, bf16[48,1152]{1,0:T(8,128)(2,1)S(1)}, u32[]{:S(2)}, u32[]{:S(2)}) %collective-permute-start.14) | collective-permute-done | bytes 110624 | tf_op jit(solution)/shard_map/ppermute | solution.py:309
  96.1 3.1 place.3.w_ref
  103.5 8.4 %attend.2 = (bf16[1024,1152]{1,0:T(8,128)(2,1)S(1)}, bf16[1024,384]{1,0:T(8,128)(2,1)S(1)}, f32[2,6,512]{2,1,0:T(8,128)S(1)}) custom-call(s32[2]{0:T(128)S(1)} %dynamic_slice.165.len_ref, bf16[1024,768]{1,0:T(8,128)(2,1)S(1)} %copy-done.5, bf16[768,1152]{1,0:T(8,128)(2,1)S(1)} %place.3.w_ref, f32[1,1152]{1,0:T(1,128)S(1)} %reshape.72.b_ref), custom_call_target="tpu_custom_call" | custom-call | flops 30000001024 | bytes 8000000 | tf_op jit(solution)/shard_map/attend/pallas_call | solution.py:90
  119.5 8.4 %attend.3 = (bf16[1024,1152]{1,0:T(8,128)(2,1)S(1)}, bf16[1024,384]{1,0:T(8,128)(2,1)S(1)}, f32[2,6,512]{2,1,0:T(8,128)S(1)}) custom-call(s32[2]{0:T(128)S(1)} %dynamic_slice.165.len_ref, bf16[1024,768]{1,0:T(8,128)(2,1)S(1)} %copy-done.5, bf16[768,1152]{1,0:T(8,128)(2,1)S(1)} %collective-permute-done.15.w_ref, f32[1,1152]{1,0:T(1,128)S(1)} %reshape.73.b_ref), custom_call_target="tpu_custom_call" | custom-call | flops 30000001024 | bytes 8000000 | tf_op jit(solution)/shard_map/attend/pallas_call | solution.py:90
  132.6 38.5 %middle.1 = (bf16[1024,768]{1,0:T(8,128)(2,1)}, bf16[1024,1536]{1,0:T(8,128)(2,1)}, bf16[1024,1536]{1,0:T(8,128)(2,1)}, bf16[1024,1536]{1,0:T(8,128)(2,1)}, bf16...) custom-call(bf16[1024,384]{1,0:T(8,128)(2,1)} %copy-done.55, ...), custom_call_target="tpu_custom_call" | custom-call | flops 60000002048 | bytes 40000000 | tf_op jit(solution)/shard_map/middle/pallas_call | solution.py:277
  173.7 10.0 %attend_back.3 = (bf16[1024,1152]{1,0:T(8,128)(2,1)S(1)}, f32[1,1152]{1,0:T(1,128)S(1)}) custom-call(s32[2]{0:T(128)S(1)} %dynamic_slice.165.len_ref, bf16[1024,1152]{1,0:T(8,128)(2,1)S(1)} %copy-done.62, f32[2,6,512]{2,1,0:T(8,128)S(1)} %get-tuple-element.53.lse_ref, bf16[1024,384]{1,0:T(8,128)(2,1)S(1)} %copy-done.64), custom_call_target="tpu_custom_call" | custom-call | flops 32000000000 | bytes 8000000 | tf_op jit(solution)/shard_map/attend_back/pallas_call | solution.py:159
  188.2 10.3 %attend_back.2 = (bf16[1024,1152]{1,0:T(8,128)(2,1)S(1)}, f32[1,1152]{1,0:T(1,128)S(1)}) custom-call(s32[2]{0:T(128)S(1)} %dynamic_slice.165.len_ref, bf16[1024,1152]{1,0:T(8,128)(2,1)S(1)} %copy-done.60, f32[2,6,512]{2,1,0:T(8,128)S(1)} %get-tuple-element.49.lse_ref, bf16[1024,384]{1,0:T(8,128)(2,1)S(1)} %copy-done.63), custom_call_target="tpu_custom_call" | custom-call | flops 32000000000 | bytes 8000000 | tf_op jit(solution)/shard_map/attend_back/pallas_call | solution.py:159
  200.0 2.8 convolution_convert_fusion.3
  216.8 3.4 %convolution_convert_fusion = bf16[768,1536]{1,0:T(8,128)(2,1)S(1)} fusion(bf16[1024,768]{1,0:T(8,128)(2,1)S(1)} %copy-done.82, bf16[1024,1536]{1,0:T(8,128)(2,1)S(1)} %copy-done.80), kind=kOutput, calls=%fused_computation.3 | convolution fusion | flops 2417098752 | bytes 7077888 | tf_op jit(solution)/shard_map/dot_general | solution.py:25
  224.6 2.9 convolution_convert_fusion.1
  230.4 2.9 collective-permute-done.61
  234.1 3.7 %collective-permute-done.62 = bf16[2,48,384]{2,1,0:T(8,128)(2,1)S(1)} collective-permute-done((bf16[2,48,384]{2,1,0:T(8,128)(2,1)S(1)}, bf16[2,48,384]{2,1,0:T(8,128)(2,1)S(1)}, u32[]{:S(2)}, u32[]{:S(2)}) %collective-permute-start.62) | collective-permute-done | bytes 73760 | tf_op jit(solution)/shard_map/ppermute | solution.py:309
  257.4 8.4 %collective-permute-done.55 = bf16[2,2,48,1152]{3,2,1,0:T(8,128)(2,1)S(1)} collective-permute-done((bf16[2,2,48,1152]{3,2,1,0:T(8,128)(2,1)S(1)}, bf16[2,2,48,1152]{3,2,1,0:T(8,128)(2,1)S(1)}, u32[]{:S(2)}, u32[]{:S(2)}) %collective-permute-start.55) | collective-permute-done | bytes 442400 | tf_op jit(solution)/shard_map/ppermute | solution.py:309
  270.2 3.0 add_convert_fusion
  275.3 3.2 add_convert_fusion.1
  279.1 3.1 collective-permute-start.58
  285.7 3.8 %collective-permute-done.58 = bf16[48,1152]{1,0:T(8,128)(2,1)S(1)} collective-permute-done((bf16[48,1152]{1,0:T(8,128)(2,1)S(1)}, bf16[48,1152]{1,0:T(8,128)(2,1)S(1)}, u32[]{:S(2)}, u32[]{:S(2)}) %collective-permute-start.58) | collective-permute-done | bytes 110624 | tf_op jit(solution)/shard_map/ppermute | solution.py:309
  294.1 8.3 %collective-permute-done.71 = bf16[2,2,48,1536]{3,2,1,0:T(8,128)(2,1)S(1)} collective-permute-done((bf16[2,2,48,1536]{3,2,1,0:T(8,128)(2,1)S(1)}, bf16[2,2,48,1536]{3,2,1,0:T(8,128)(2,1)S(1)}, u32[]{:S(2)}, u32[]{:S(2)}) %collective-permute-start.71) | collective-permute-done | bytes 589856 | tf_op jit(solution)/shard_map/ppermute | solution.py:309
  306.5 3.4 %collective-permute-done.80 = bf16[2,48,1536]{2,1,0:T(8,128)(2,1)S(1)} collective-permute-done((bf16[2,48,1536]{2,1,0:T(8,128)(2,1)S(1)}, bf16[2,48,1536]{2,1,0:T(8,128)(2,1)S(1)}, u32[]{:S(2)}, u32[]{:S(2)}) %collective-permute-start.80) | collective-permute-done | bytes 294944 | tf_op jit(solution)/shard_map/ppermute | solution.py:309
  320.9 3.5 %collective-permute-done.82 = bf16[48,1536]{1,0:T(8,128)(2,1)S(1)} collective-permute-done((bf16[48,1536]{1,0:T(8,128)(2,1)S(1)}, bf16[48,1536]{1,0:T(8,128)(2,1)S(1)}, u32[]{:S(2)}, u32[]{:S(2)}) %collective-permute-start.82) | collective-permute-done | bytes 147488 | tf_op jit(solution)/shard_map/ppermute | solution.py:309
  325.3 7.8 %collective-permute-done.74 = bf16[48,1536]{1,0:T(8,128)(2,1)S(1)} collective-permute-done((bf16[48,1536]{1,0:T(8,128)(2,1)S(1)}, bf16[48,1536]{1,0:T(8,128)(2,1)S(1)}, u32[]{:S(2)}, u32[]{:S(2)}) %collective-permute-start.74) | collective-permute-done | bytes 147488 | tf_op jit(solution)/shard_map/ppermute | solution.py:309
  (435 shorter events, 169.1 us)
Async XLA Ops:
  32.0 15.0 %collective-permute-start.24 = (bf16[48,1920]{1,0:T(8,128)(2,1)S(1)}, bf16[48,1920]{1,0:T(8,128)(2,1)}, u32[]{:S(2)}, u32[]{:S(2)}) collective-permute-start(bf16[48,1920]{1,0:T(8,128)(2,1)S(1)} %pad_maximum_fusion.2.refs_0_), channel_id=1, source_target_pairs={{0,16},{2,18},{4,20},{6,22},{8,24},{10,26},{12,28},{14,30},{16,0},... | collective-permute-start | bytes 552968 | tf_op jit(solution)/shard_map/ppermute | solution.py:309
  32.0 16.1 %collective-permute-start.28 = (bf16[48,1920]{1,0:T(8,128)(2,1)S(1)}, bf16[48,1920]{1,0:T(8,128)(2,1)}, u32[]{:S(2)}, u32[]{:S(2)}) collective-permute-start(bf16[48,1920]{1,0:T(8,128)(2,1)S(1)} %pad_maximum_fusion.2.refs_0_), channel_id=1, source_target_pairs={{0,24},{2,26},{4,28},{6,30},{8,16},{10,18},{12,20},{14,22},{16,8},... | collective-permute-start | bytes 552968 | tf_op jit(solution)/shard_map/ppermute | solution.py:309
  34.5 15.1 %collective-permute-start.18 = (bf16[48,1920]{1,0:T(8,128)(2,1)S(1)}, bf16[48,1920]{1,0:T(8,128)(2,1)S(1)}, u32[]{:S(2)}, u32[]{:S(2)}) collective-permute-start(bf16[48,1920]{1,0:T(8,128)(2,1)S(1)} %pad_maximum_fusion.2.refs_0_), channel_id=1, source_target_pairs={{0,4},{2,6},{4,0},{6,2},{8,12},{10,14},{12,8},{14,10},{16,20},{18,... | collective-permute-start | bytes 552968 | tf_op jit(solution)/shard_map/ppermute | solution.py:309
  68.2 17.8 %collective-permute-start.22 = (bf16[48,1920]{1,0:T(8,128)(2,1)}, bf16[48,1920]{1,0:T(8,128)(2,1)}, u32[]{:S(2)}, u32[]{:S(2)}) collective-permute-start(bf16[48,1920]{1,0:T(8,128)(2,1)} %copy-done.9), channel_id=1, source_target_pairs={{0,4},{2,6},{4,0},{6,2},{8,12},{10,14},{12,8},{14,10},{16,20},{18,... | collective-permute-start | bytes 552968 | tf_op jit(solution)/shard_map/ppermute | solution.py:309
  70.5 19.3 %collective-permute-start.21 = (bf16[48,1920]{1,0:T(8,128)(2,1)}, bf16[48,1920]{1,0:T(8,128)(2,1)S(1)}, u32[]{:S(2)}, u32[]{:S(2)}) collective-permute-start(bf16[48,1920]{1,0:T(8,128)(2,1)} %copy-done.9), channel_id=1, source_target_pairs={{0,2},{2,0},{4,6},{6,4},{8,10},{10,8},{12,14},{14,12},{16,18},{18,... | collective-permute-start | bytes 552968 | tf_op jit(solution)/shard_map/ppermute | solution.py:309
  86.0 15.3 %collective-permute-start.30 = (bf16[48,1920]{1,0:T(8,128)(2,1)}, bf16[48,1920]{1,0:T(8,128)(2,1)}, u32[]{:S(2)}, u32[]{:S(2)}) collective-permute-start(bf16[48,1920]{1,0:T(8,128)(2,1)} %collective-permute-done.28.refs_12_), channel_id=1, source_target_pairs={{0,4},{2,6},{4,0},{6,2},{8,12},{10,14},{12,8},{14,10},{16,20},{18,... | collective-permute-start | bytes 552968 | tf_op jit(solution)/shard_map/ppermute | solution.py:309
  99.3 17.2 %collective-permute-start.19 = (bf16[48,1920]{1,0:T(8,128)(2,1)}, bf16[48,1920]{1,0:T(8,128)(2,1)S(1)}, u32[]{:S(2)}, u32[]{:S(2)}) collective-permute-start(bf16[48,1920]{1,0:T(8,128)(2,1)} %copy-done.11), channel_id=1, source_target_pairs={{0,2},{2,0},{4,6},{6,4},{8,10},{10,8},{12,14},{14,12},{16,18},{18,... | collective-permute-start | bytes 552968 | tf_op jit(solution)/shard_map/ppermute | solution.py:309
  101.3 18.2 %collective-permute-start.15 = (bf16[768,1152]{1,0:T(8,128)(2,1)S(1)}, bf16[768,1152]{1,0:T(8,128)(2,1)S(1)}, u32[]{:S(2)}, u32[]{:S(2)}) collective-permute-start(bf16[768,1152]{1,0:T(8,128)(2,1)S(1)} %place.3.w_ref), channel_id=1, source_target_pairs={{0,1},{1,0},{2,3},{3,2},{4,5},{5,4},{6,7},{7,6},{8,9},{9,8},{10,11... | collective-permute-start | bytes 5308424 | tf_op jit(solution)/shard_map/ppermute | solution.py:305
  101.3 15.3 %collective-permute-start.23 = (bf16[48,1920]{1,0:T(8,128)(2,1)}, bf16[48,1920]{1,0:T(8,128)(2,1)S(1)}, u32[]{:S(2)}, u32[]{:S(2)}) collective-permute-start(bf16[48,1920]{1,0:T(8,128)(2,1)} %collective-permute-done.22.refs_6_), channel_id=1, source_target_pairs={{0,2},{2,0},{4,6},{6,4},{8,10},{10,8},{12,14},{14,12},{16,18},{18,... | collective-permute-start | bytes 552968 | tf_op jit(solution)/shard_map/ppermute | solution.py:309
  101.5 15.1 %collective-permute-start.27 = (bf16[48,1920]{1,0:T(8,128)(2,1)S(1)}, bf16[48,1920]{1,0:T(8,128)(2,1)S(1)}, u32[]{:S(2)}, u32[]{:S(2)}) collective-permute-start(bf16[48,1920]{1,0:T(8,128)(2,1)S(1)} %copy-done.18), channel_id=1, source_target_pairs={{0,4},{2,6},{4,0},{6,2},{8,12},{10,14},{12,8},{14,10},{16,20},{18,... | collective-permute-start | bytes 552968 | tf_op jit(solution)/shard_map/ppermute | solution.py:309
  185.2 20.5 %collective-permute-start.84 = (f32[7296]{0:T(1024)S(1)}, f32[7296]{0:T(1024)S(1)}, u32[]{:S(2)}, u32[]{:S(2)}) collective-permute-start(f32[7296]{0:T(1024)S(1)} %pad_maximum_fusion.4), channel_id=1, source_target_pairs={{0,1},{1,0},{2,3},{3,2},{4,5},{5,4},{6,7},{7,6},{8,9},{9,8},{10,11... | collective-permute-start | bytes 87560 | tf_op jit(solution)/shard_map/ppermute | solution.py:305
  202.8 19.6 %collective-permute-start.60 = (bf16[768,384]{1,0:T(8,128)(2,1)S(1)}, bf16[768,384]{1,0:T(8,128)(2,1)S(1)}, u32[]{:S(2)}, u32[]{:S(2)}) collective-permute-start(bf16[768,384]{1,0:T(8,128)(2,1)S(1)} %convolution_convert_fusion.3), channel_id=1, source_target_pairs={{0,1},{1,0},{2,3},{3,2},{4,5},{5,4},{6,7},{7,6},{8,9},{9,8},{10,11... | collective-permute-start | bytes 1769480 | tf_op jit(solution)/shard_map/ppermute | solution.py:305
  205.5 45.2 %collective-permute-start.52 = (bf16[768,1152]{1,0:T(8,128)(2,1)S(1)}, bf16[768,1152]{1,0:T(8,128)(2,1)S(1)}, u32[]{:S(2)}, u32[]{:S(2)}) collective-permute-start(bf16[768,1152]{1,0:T(8,128)(2,1)S(1)} %convolution_convert_fusion.2), channel_id=1, source_target_pairs={{0,1},{1,0},{2,3},{3,2},{4,5},{5,4},{6,7},{7,6},{8,9},{9,8},{10,11... | collective-permute-start | bytes 5308424 | tf_op jit(solution)/shard_map/ppermute | solution.py:305
  213.6 34.8 %collective-permute-start.51 = (bf16[1024,768]{1,0:T(8,128)(2,1)S(1)}, bf16[1024,768]{1,0:T(8,128)(2,1)S(1)}, u32[]{:S(2)}, u32[]{:S(2)}) collective-permute-start(bf16[1024,768]{1,0:T(8,128)(2,1)S(1)} %add_convert_fusion.2), channel_id=1, source_target_pairs={{0,1},{1,0},{2,3},{3,2},{4,5},{5,4},{6,7},{7,6},{8,9},{9,8},{10,11... | collective-permute-start | bytes 4718600 | tf_op jit(solution)/shard_map/ppermute | solution.py:305
  213.6 36.8 %collective-permute-start.50 = (bf16[1024,768]{1,0:T(8,128)(2,1)S(1)}, bf16[1024,768]{1,0:T(8,128)(2,1)S(1)}, u32[]{:S(2)}, u32[]{:S(2)}) collective-permute-start(bf16[1024,768]{1,0:T(8,128)(2,1)S(1)} %copy-done.65), channel_id=1, source_target_pairs={{0,1},{1,0},{2,3},{3,2},{4,5},{5,4},{6,7},{7,6},{8,9},{9,8},{10,11... | collective-permute-start | bytes 4718600 | tf_op jit(solution)/shard_map/ppermute | solution.py:305
  245.2 24.9 %collective-permute-start.76 = (bf16[768,1536]{1,0:T(8,128)(2,1)S(1)}, bf16[768,1536]{1,0:T(8,128)(2,1)S(1)}, u32[]{:S(2)}, u32[]{:S(2)}) collective-permute-start(bf16[768,1536]{1,0:T(8,128)(2,1)S(1)} %convolution_convert_fusion), channel_id=1, source_target_pairs={{0,1},{1,0},{2,3},{3,2},{4,5},{5,4},{6,7},{7,6},{8,9},{9,8},{10,11... | collective-permute-start | bytes 7077896 | tf_op jit(solution)/shard_map/ppermute | solution.py:305
  247.6 27.7 %collective-permute-start.68 = (bf16[768,1536]{1,0:T(8,128)(2,1)S(1)}, bf16[768,1536]{1,0:T(8,128)(2,1)S(1)}, u32[]{:S(2)}, u32[]{:S(2)}) collective-permute-start(bf16[768,1536]{1,0:T(8,128)(2,1)S(1)} %convolution_convert_fusion.1), channel_id=1, source_target_pairs={{0,1},{1,0},{2,3},{3,2},{4,5},{5,4},{6,7},{7,6},{8,9},{9,8},{10,11... | collective-permute-start | bytes 7077896 | tf_op jit(solution)/shard_map/ppermute | solution.py:305
  273.4 18.3 %collective-permute-start.79 = (bf16[2,2,48,1536]{3,2,1,0:T(8,128)(2,1)S(1)}, bf16[2,2,48,1536]{3,2,1,0:T(8,128)(2,1)S(1)}, u32[]{:S(2)}, u32[]{:S(2)}) collective-permute-start(bf16[2,2,48,1536]{3,2,1,0:T(8,128)(2,1)S(1)} %dynamic-slice_bitcast_fusion), channel_id=1, source_target_pairs={{0,4},{2,6},{4,0},{6,2},{8,12},{10,14},{12,8},{14,10},{16,20},{18,... | collective-permute-start | bytes 1769480 | tf_op jit(solution)/shard_map/ppermute | solution.py:309
  273.6 18.9 %collective-permute-start.77 = (bf16[2,2,48,1536]{3,2,1,0:T(8,128)(2,1)S(1)}, bf16[2,2,48,1536]{3,2,1,0:T(8,128)(2,1)S(1)}, u32[]{:S(2)}, u32[]{:S(2)}) collective-permute-start(bf16[2,2,48,1536]{3,2,1,0:T(8,128)(2,1)S(1)} %dynamic-slice_bitcast_fusion.1), channel_id=1, source_target_pairs={{0,2},{2,0},{4,6},{6,4},{8,10},{10,8},{12,14},{14,12},{16,18},{18,... | collective-permute-start | bytes 1769480 | tf_op jit(solution)/shard_map/ppermute | solution.py:309
  283.8 18.5 %collective-permute-start.71 = (bf16[2,2,48,1536]{3,2,1,0:T(8,128)(2,1)S(1)}, bf16[2,2,48,1536]{3,2,1,0:T(8,128)(2,1)S(1)}, u32[]{:S(2)}, u32[]{:S(2)}) collective-permute-start(bf16[2,2,48,1536]{3,2,1,0:T(8,128)(2,1)S(1)} %dynamic-slice_bitcast_fusion.2), channel_id=1, source_target_pairs={{0,4},{2,6},{4,0},{6,2},{8,12},{10,14},{12,8},{14,10},{16,20},{18,... | collective-permute-start | bytes 1769480 | tf_op jit(solution)/shard_map/ppermute | solution.py:309
  289.5 16.3 %collective-permute-start.69 = (bf16[2,2,48,1536]{3,2,1,0:T(8,128)(2,1)S(1)}, bf16[2,2,48,1536]{3,2,1,0:T(8,128)(2,1)S(1)}, u32[]{:S(2)}, u32[]{:S(2)}) collective-permute-start(bf16[2,2,48,1536]{3,2,1,0:T(8,128)(2,1)S(1)} %dynamic-slice_bitcast_fusion.3), channel_id=1, source_target_pairs={{0,2},{2,0},{4,6},{6,4},{8,10},{10,8},{12,14},{14,12},{16,18},{18,... | collective-permute-start | bytes 1769480 | tf_op jit(solution)/shard_map/ppermute | solution.py:309
  291.8 18.1 %collective-permute-start.80 = (bf16[2,48,1536]{2,1,0:T(8,128)(2,1)S(1)}, bf16[2,48,1536]{2,1,0:T(8,128)(2,1)S(1)}, u32[]{:S(2)}, u32[]{:S(2)}) collective-permute-start(bf16[2,48,1536]{2,1,0:T(8,128)(2,1)S(1)} %dynamic-slice_bitcast_fusion.6), channel_id=1, source_target_pairs={{0,2},{2,0},{4,6},{6,4},{8,10},{10,8},{12,14},{14,12},{16,18},{18,... | collective-permute-start | bytes 884744 | tf_op jit(solution)/shard_map/ppermute | solution.py:309
  292.7 17.3 %collective-permute-start.78 = (bf16[2,48,1536]{2,1,0:T(8,128)(2,1)S(1)}, bf16[2,48,1536]{2,1,0:T(8,128)(2,1)S(1)}, u32[]{:S(2)}, u32[]{:S(2)}) collective-permute-start(bf16[2,48,1536]{2,1,0:T(8,128)(2,1)S(1)} %dynamic-slice_bitcast_fusion.7), channel_id=1, source_target_pairs={{0,4},{2,6},{4,0},{6,2},{8,12},{10,14},{12,8},{14,10},{16,20},{18,... | collective-permute-start | bytes 884744 | tf_op jit(solution)/shard_map/ppermute | solution.py:309
  315.0 18.0 %collective-permute-start.74 = (bf16[48,1536]{1,0:T(8,128)(2,1)S(1)}, bf16[48,1536]{1,0:T(8,128)(2,1)S(1)}, u32[]{:S(2)}, u32[]{:S(2)}) collective-permute-start(bf16[48,1536]{1,0:T(8,128)(2,1)S(1)} %get-tuple-element.83), channel_id=1, source_target_pairs={{0,16},{2,18},{4,20},{6,22},{8,24},{10,26},{12,28},{14,30},{16,0},... | collective-permute-start | bytes 442376 | tf_op jit(solution)/shard_map/ppermute | solution.py:309
  (152 other events, 1459.5 us)
